TPU v7x, 128 devices: a whole 4x4x4 slice. The times are simulated.
128 devices in a mesh: rep: 16 (over y, z), tm: 8 (over x, core).
Axes of the slice: x: 4, y: 4, z: 4, core: 2. Of those that a mesh axis runs over, the one named last changes fastest.
Arguments:
- video: bfloat16 [16, 32, 16, 32, 128], P('rep', 'tm'), may hold values from -6 to 6
- frame_counts: int32 [16], P('rep'), may hold values from 1 to 32, as said below
- first_weight: bfloat16 [3, 3, 3, 256, 256], replicated, may hold values from -0.078125 to 0.078125
- second_weight: bfloat16 [3, 512, 512], replicated, may hold values from -0.15625 to 0.15625
- cotangent: bfloat16 [16, 8, 16, 32, 512], P('rep', None, 'tm'), may hold values from -6 to 6
Outputs:
- features_out: bfloat16 [16, 8, 16, 32, 512], P('rep', None, 'tm')
- grad_input: bfloat16 [16, 32, 16, 32, 128], P('rep', 'tm')
- grad_first: float32 [6912, 256], P('rep')
- grad_second: float32 [1536, 512], P('rep')
Inputs may be any that keep to these rules, and one draw needn't show every extreme that they name: `frame_counts`: at least one clip has exactly 32 live frames.
All inputs are finite; a program needn't handle non-finite values.
Results may differ from a plain program's by a relative error of at most 0.013.
Values may be sent and summed in bfloat16 or wider, within the bound.
A program may use at most 128 MiB of HBM per device.

v0:
```python
import functools
import math

import jax
import jax.numpy as jnp
from jax import lax
from jax.experimental import pallas as pl
from jax.experimental.pallas import tpu as pltpu
from jax.sharding import PartitionSpec as P

root_half = 0.7071067811865476
MESH = pl.DeviceIdType.MESH
bf16 = jnp.bfloat16
f32 = jnp.float32

NY, NZ, NX = 4, 4, 4
ROWS_F, ROWS_S = 432, 96


def dot(a, b):
    return jnp.dot(a, b, preferred_element_type=f32)


def dot_nt(a, b):
    return lax.dot_general(a, b, (((1,), (1,)), ((), ())), preferred_element_type=f32)


def repeat(count, step):
    def run(i, carry):
        step(i)
        return carry

    lax.fori_loop(0, count, run, 0)


def put_shifted(dst, frame, rows, value, flip):
    lanes = (512, 0) if flip else (0, 512)
    wide = value.astype(f32)
    column = lax.broadcasted_iota(jnp.int32, wide.shape, 1)
    before = jnp.where(column == 0, 0.0, pltpu.roll(wide, 1, 1)).astype(bf16)
    after = jnp.where(column == 31, 0.0, pltpu.roll(wide, 31, 1)).astype(bf16)
    dst[frame, rows, :, lanes[0] : lanes[0] + 256] = before
    dst[frame, rows, :, 256:512] = value
    dst[frame, rows, :, lanes[1] : lanes[1] + 256] = after


def kernel(
    video, counts, first_w, second_w, cotangent,
    feat_out, input_out, first_sums, second_sums,
    vid, w1, w1t, w2, ctp, cts, ct_t, hown, win, xs, acc, gh, sh,
    gpc, gph, gp_t, gpx, pf, r1a, r1b, s1a, s1b, r2a, r2b, s2, r3, ag,
    px, q1, t1, q2, t2, q3, t3, ags, fout, gsend, gout,
    load_sem, win_s, win_r, ed_s, ed_r, fw_s, fw_r, cts_s, cts_r, sh_s, sh_r,
    gp_s, gp_r, gph_s, gph_r, gi_s, gi_r, f1_s, f1a_r, f1b_r, p2a_s, p2a_r, p2b_s, p2b_r,
    p3_s, p3_r, p4_s, p4_r, q1_s, q1_r, q2_s, q2_r, q3_s, q3_r, q4_s, q4_r, out_sem,
):
    rep = lax.axis_index("rep")
    tm = lax.axis_index("tm")
    y, z = rep // NZ, rep % NZ
    x, c = tm // 2, tm % 2

    def remote(src, dst, send, recv, to):
        return pltpu.make_async_remote_copy(
            src_ref=src, dst_ref=dst, send_sem=send, recv_sem=recv, device_id=to, device_id_type=MESH
        )

    def device(to_x, to_y, to_z, to_c):
        return (to_y * NZ + to_z, to_x * 2 + to_c)

    sibling = (rep, x * 2 + 1 - c)

    loads = [
        pltpu.make_async_copy(video, vid, load_sem.at[0]),
        pltpu.make_async_copy(cotangent, ctp.at[pl.ds(0, 8)], load_sem.at[1]),
        pltpu.make_async_copy(second_w, w2, load_sem.at[2]),
        pltpu.make_async_copy(first_w, w1, load_sem.at[3]),
    ]
    for load in loads:
        load.start()

    barrier = pltpu.get_barrier_semaphore()

    def greet(to):
        pl.semaphore_signal(barrier, inc=1, device_id=to, device_id_type=MESH)

    repeat(7, lambda i: greet((rep, (tm + 1 + i) % 8)))
    repeat(3, lambda i: greet(device(x, (y + 1 + i) % NY, z, c)))
    repeat(3, lambda i: greet(device(x, y, (z + 1 + i) % NZ, c)))

    live = counts[0]
    loads[0].wait()

    def keep(frame):
        return jnp.where(tm * 4 + frame < live, 1.0, 0.0).astype(f32)

    for t in range(2):
        even, odd = keep(2 * t), keep(2 * t + 1)
        hown[t, 0:32] = jnp.zeros((32, 256), bf16)
        hown[t, 544:576] = jnp.zeros((32, 256), bf16)

        def pair(n, carry):
            at = pl.ds(pl.multiple_of(n * 64, 64), 64)
            to = pl.ds(pl.multiple_of(n * 64 + 32, 32), 64)
            one = vid[2 * t, at].astype(f32) * even
            two = vid[2 * t + 1, at].astype(f32) * odd
            hown[t, to, 0:128] = ((one + two) * root_half).astype(bf16)
            hown[t, to, 128:256] = ((one - two) * root_half).astype(bf16)
            return carry

        lax.fori_loop(0, 8, pair, 0)

    pl.semaphore_wait(barrier, 13)

    def window_rows(core):
        return pl.ds(pl.multiple_of(96 * core, 32), 96)

    def frames_of(source):
        return pl.ds(2 * source, 2)

    def in_turn(i):
        step = i // 2
        return (x + step + step // 2 - 2 * (step // 3)) % 4 * 2 + (c + i) % 2

    def spread(i):
        to = in_turn((i + 1) % 8)
        rows = pl.ds(pl.multiple_of(32 * (4 * (to // 2) + 3 * (to % 2)), 32), 96)
        return remote(
            hown.at[:, rows],
            win.at[frames_of(tm), window_rows(to % 2)],
            win_s.at[to],
            win_r.at[tm],
            (rep, to),
        )

    repeat(7, lambda i: spread((i + 1) % 7).start())
    win[frames_of(tm), window_rows(c)] = hown[
        :, pl.ds(pl.multiple_of(32 * (4 * x + 3 * c), 32), 96)
    ]

    def edge_rows(core):
        return pl.ds(pl.multiple_of(64 + 32 * core, 32), 32)

    def rest_rows(core):
        return pl.ds(pl.multiple_of(128 * core, 32), 64)

    def hand_edge(source):
        block = win.at[frames_of(source), edge_rows(c)]
        return remote(block, block, ed_s.at[source], ed_r.at[source], sibling)

    def hand_rest(source):
        block = win.at[frames_of(source), rest_rows(c)]
        return remote(block, block, fw_s.at[source], fw_r.at[source], sibling)

    loads[1].wait()
    give_ct = remote(ctp.at[pl.ds(0, 8)], cts, cts_s, cts_r, sibling)
    give_ct.start()

    ctp[8:10] = jnp.zeros((2, 64, 512), bf16)
    loads[2].wait()

    def back_step(n, carry):
        grad = jnp.zeros((256, 512), f32)
        for a in range(3):
            grad = grad + dot_nt(ctp[pl.ds(4 * n + 2 - a, 4)].reshape(256, 512), w2[a])
        low, high = grad[:, :256], grad[:, 256:]
        gh[pl.ds(4 * n, 4), 0] = ((low + high) * root_half).astype(bf16).reshape(4, 64, 256)
        gh[pl.ds(4 * n, 4), 1] = ((low - high) * root_half).astype(bf16).reshape(4, 64, 256)
        return carry

    lax.fori_loop(0, 2, back_step, 0)

    loads[3].wait()

    def turn_tap(n, carry):
        for d in range(3):
            w1t[n, 256 * d : 256 * d + 256] = w1[n, 256 * d : 256 * d + 256].T
        return carry

    lax.fori_loop(0, 9, turn_tap, 0)
    ct_t[:, 0:512] = ctp[0:8].reshape(512, 512).T
    xs[0:2] = jnp.zeros((2, 6, 32, 768), bf16)
    gpx[16:18] = jnp.zeros((2, 4, 32, 768), bf16)
    for j in range(2):
        sh[j, 0:2] = jnp.zeros((2, 64, 512), bf16)
    acc[...] = jnp.zeros_like(acc)

    def take(source, row, count):
        for t in range(2):
            frame = 2 * source + t
            block = win[frame, pl.ds(pl.multiple_of(32 * row, 32), 32 * count)]
            put_shifted(xs, 2 + frame, pl.ds(row, count), block.reshape(count, 32, 256), False)

    def from_afar(i):
        source = in_turn(i)

        @pl.when(source != tm)
        def _():
            block = win.at[frames_of(source), window_rows(c)]
            remote(block, block, win_r.at[source], win_r.at[source], sibling).wait_recv()

        hand_edge(source).start()
        take(source, 3 * c, 3)

    def from_sibling(i):
        source = in_turn(i)
        hand_rest(source).start()
        block = win.at[frames_of(source), edge_rows(1 - c)]
        remote(block, block, ed_r.at[source], ed_r.at[source], sibling).wait_recv()
        take(source, 3 - c, 1)

    repeat(8, from_afar)
    repeat(8, from_sibling)

    def taps(n, carry):
        a, b = n // 3, n % 3
        acc[...] += dot(xs[pl.ds(a, 16), pl.ds(2 * c + b, 2)].reshape(1024, 768), w1[n])
        return carry

    lax.fori_loop(0, 9, taps, 0, unroll=9)

    def activate(n, carry):
        hidden = []
        for t in range(2):
            value = acc[pl.ds(pl.multiple_of(n * 128 + 64 * t, 64), 64)]
            gate = jax.nn.sigmoid(value)
            hidden.append((value * gate).astype(bf16).astype(f32))
            grad = gh[n, t].astype(f32) * (gate * (1.0 + value * (1.0 - gate)))
            gpc[2 * n + t, pl.ds(2 * c, 2)] = grad.astype(bf16).reshape(2, 32, 256)
        sh[0, 2 + n, :, 0:256] = ((hidden[0] + hidden[1]) * root_half).astype(bf16)
        sh[0, 2 + n, :, 256:512] = ((hidden[0] - hidden[1]) * root_half).astype(bf16)
        return carry

    lax.fori_loop(0, 8, activate, 0)
    own_rows = gpc.at[:, pl.ds(2 * c, 2)]
    give_gp = remote(own_rows, own_rows, gp_s, gp_r, sibling)
    give_gp.start()
    give_sh = remote(sh.at[0, pl.ds(2, 8)], sh.at[1, pl.ds(2, 8)], sh_s, sh_r, sibling)
    give_sh.start()
    give_gph = remote(gpc.at[:, 3 * c], gph, gph_s, gph_r, (rep, (tm + 7 + 2 * c) % 8))
    give_gph.start()

    def turn_rows(core):
        at = pl.ds(pl.multiple_of(core * 1024, 1024), 1024)
        gp_t[:, at] = gpc[:, pl.ds(2 * core, 2)].reshape(1024, 256).T

    turn_rows(c)

    def forward(n):
        value = jnp.zeros((256, 512), f32)
        for a in range(3):
            value = value + dot(sh[0, pl.ds(4 * n + a, 4)].reshape(256, 512), w2[a])
        fout[pl.ds(4 * n, 4)] = value.astype(bf16).reshape(4, 64, 512)

    repeat(2, forward)
    write_feat = pltpu.make_async_copy(fout, feat_out, out_sem.at[0])
    write_feat.start()

    def deliver(source, shard):
        to_y, to_z = 2 * c + shard // 4, shard % 4
        stops = (
            (0, r1a.at[y, to_z], device(x, to_y, z, c), f1a_r.at[y, to_z], to_y == y),
            (1, r1b.at[z, shard // 4], device(x, y, to_z, c), f1b_r.at[z, shard // 4], to_z == z),
        )
        for half, slot, to, sem, here in stops:

            @pl.when(here)
            def _(half=half, slot=slot, sem=sem):
                pltpu.make_async_copy(source(half, shard), slot, sem).start()

            @pl.when(jnp.logical_not(here))
            def _(half=half, slot=slot, sem=sem, to=to):
                remote(source(half, shard), slot, f1_s.at[half, shard], sem, to).start()

    def delivered(source, shard):
        to_y, to_z = 2 * c + shard // 4, shard % 4
        for half, here in ((0, to_y == y), (1, to_z == z)):

            @pl.when(jnp.logical_not(here))
            def _(half=half):
                remote(
                    source(half, shard), r1a.at[0, 0], f1_s.at[half, shard], f1_s.at[half, shard], sibling
                ).wait_send()

    def source_f(half, shard):
        return pf.at[half, pl.ds(pl.multiple_of(128 + ROWS_F * shard, 16), ROWS_F)]

    give_gp.wait_recv()
    turn_rows(1 - c)

    def rest_from_sibling(source):
        block = win.at[frames_of(source), rest_rows(1 - c)]
        remote(block, block, fw_r.at[source], fw_r.at[source], sibling).wait_recv()
        take(source, 4 - 4 * c, 2)

    repeat(8, rest_from_sibling)

    def tap(j):
        k = 13 * c + j
        a, b, d = k // 9, (k // 3) % 3, k % 3
        lanes = pl.ds(pl.multiple_of(d * 256, 256), 256)
        upper = xs[pl.ds(a, 16), pl.ds(b, 2), :, lanes].reshape(1024, 256)
        lower = xs[pl.ds(a, 16), pl.ds(b + 2, 2), :, lanes].reshape(1024, 256)
        turned = (dot(gp_t[:, 0:1024], upper) + dot(gp_t[:, 1024:2048], lower)).T.astype(bf16)
        at = pl.ds(pl.multiple_of(256 * j + 128 - 128 * c, 128), 256)
        pf[0, at] = turned[:, :128]
        pf[1, at] = turned[:, 128:]

    odd_row = y % 2

    def send_shards(low):
        repeat(4, lambda k: deliver(source_f, 4 * low + (z + 1 + k) % 4))

    def first_taps(i, carry):
        tap(6 * odd_row + i)
        return carry

    lax.fori_loop(0, 8, first_taps, 0, unroll=4)
    send_shards(odd_row)

    give_ct.wait_recv()
    ct_t[:, 512:1024] = cts[...].reshape(512, 512).T
    give_sh.wait_recv()

    def stop_x(n, k):
        to = (x + k) % 4
        at = pl.ds(pl.multiple_of(256 * n, 256), 256)
        return remote(px.at[to, at], q1.at[x, at], q1_s.at[n, to], q1_r.at[n, x], (rep, 2 * to + c))

    def second_rows(n):
        m = 3 * c + n
        a, band = m // 2, m % 2
        lanes = pl.ds(pl.multiple_of(band * 256, 256), 256)
        own = sh[0, pl.ds(a, 8), :, lanes].reshape(512, 256)
        other = sh[1, pl.ds(a, 8), :, lanes].reshape(512, 256)
        turned = (dot(ct_t[:, 0:512], own) + dot(ct_t[:, 512:1024], other)).T.astype(bf16)
        at = pl.ds(pl.multiple_of(256 * n, 256), 256)
        for to_x in range(4):
            px[to_x, at] = turned[:, 128 * to_x : 128 * to_x + 128]
        repeat(3, lambda k: stop_x(n, k + 1).start())

    repeat(3, second_rows)
    q1[x] = px[x]

    def last_taps(i, carry):
        tap(8 - 8 * odd_row + i)
        return carry

    lax.fori_loop(0, 6, last_taps, 0, unroll=3)
    send_shards(1 - odd_row)

    give_gph.wait_recv()
    inner = jnp.where((c == 0) & (x == 0) | (c == 1) & (x == 3), 0.0, 1.0).astype(bf16)

    def widen(frame, carry):
        put_shifted(gpx, frame, pl.ds(1 - c, 3), gpc[frame, pl.ds(c, 3)], True)
        put_shifted(gpx, frame, pl.ds(3 * c, 1), gph[pl.ds(frame, 1)] * inner, True)
        return carry

    lax.fori_loop(0, 16, widen, 0)
    acc[...] = jnp.zeros_like(acc)

    def input_taps(n, carry):
        a, b = n // 3, n % 3
        acc[...] += dot(gpx[pl.ds(2 - a, 16), pl.ds(2 - b, 2)].reshape(1024, 768), w1t[n])
        return carry

    lax.fori_loop(0, 9, input_taps, 0, unroll=3)

    def unpair(n, carry):
        for t in range(2):
            at = pl.ds(pl.multiple_of(n * 128 + 64 * t, 64), 64)
            low, high = acc[at, 0:128], acc[at, 128:256]
            even = jnp.where(4 * n + 2 * t < live, 1.0, 0.0).astype(f32)
            odd = jnp.where(4 * n + 2 * t + 1 < live, 1.0, 0.0).astype(f32)
            gsend[n, 2 * t] = ((low + high) * root_half * even).astype(bf16)
            gsend[n, 2 * t + 1] = ((low - high) * root_half * odd).astype(bf16)
        return carry

    lax.fori_loop(0, 8, unpair, 0)

    def pixel_rows(source):
        return gout.at[:, pl.ds(pl.multiple_of(64 * source, 64), 64)]

    def give_back(i):
        to = in_turn(i + 1)
        return remote(gsend.at[to], pixel_rows(tm), gi_s.at[to], gi_r.at[tm], (rep, to))

    repeat(7, lambda i: give_back(6 - i).start())
    gout[:, pl.ds(pl.multiple_of(64 * tm, 64), 64)] = gsend[tm]

    owner = c == y // 2

    def peer_of(i, home):
        return (home + 1 + i) % 4

    def wait_for(slot, sem):
        remote(slot, slot, sem, sem, sibling).wait_recv()

    def from_x(i):
        n, peer = i // 3, peer_of(i % 3, x)
        wait_for(q1.at[peer, pl.ds(pl.multiple_of(256 * n, 256), 256)], q1_r.at[n, peer])

    repeat(9, from_x)

    def four(ref, *index):
        total = ref[(0,) + index].astype(f32)
        for source in range(1, 4):
            total = total + ref[(source,) + index].astype(f32)
        return total.astype(bf16)

    def sum_x(i, carry):
        t1[i] = four(q1, pl.ds(pl.multiple_of(96 * i, 16), 96))
        return carry

    lax.fori_loop(0, 8, sum_x, 0)

    def give_y(i):
        return remote(
            t1.at[pl.ds(4 * i, 4)], q2.at[y], q2_s.at[i], q2_r.at[y], device(x, 2 * c + i, z, c)
        )

    def start_y(i):
        @pl.when(2 * c + i != y)
        def _():
            give_y(i).start()

        @pl.when(2 * c + i == y)
        def _():
            q2[y] = t1[pl.ds(4 * i, 4)]

    repeat(2, start_y)

    def landed(slot, sem):
        pltpu.make_async_copy(slot, slot, sem).wait()

    def give_b(i):
        return remote(s1b.at[i], r2b.at[y], p2b_s.at[i], p2b_r.at[y], device(x, 2 * c + i, z, c))

    def give_a(k):
        return remote(s1a.at[k], r2a.at[z], p2a_s.at[k], p2a_r.at[z], device(x, y, k, c))

    def give_z(k):
        return remote(t2.at[k], q3.at[z], q3_s.at[k], q3_r.at[z], device(x, y, k, c))

    def sum_b(i):
        repeat(4, lambda source: landed(r1b.at[source, i], f1b_r.at[source, i]))
        s1b[i] = four(r1b, i)

        @pl.when(2 * c + i != y)
        def _():
            give_b(i).start()

        @pl.when(2 * c + i == y)
        def _():
            r2b[y] = s1b[i]

    sum_b(odd_row)

    @pl.when(owner)
    def _():
        def sum_a(k):
            repeat(4, lambda source: landed(r1a.at[source, k], f1a_r.at[source, k]))
            s1a[k] = four(r1a, k)

            @pl.when(k != z)
            def _():
                give_a(k).start()

        repeat(4, lambda k: sum_a((z + 1 + k) % 4))
        r2a[z] = s1a[z]

    sum_b(1 - odd_row)

    @pl.when(owner)
    def _():
        repeat(3, lambda i: wait_for(q2.at[peer_of(i, y)], q2_r.at[peer_of(i, y)]))

        def sum_y(k):
            t2[k] = four(q2, k)

            @pl.when(k != z)
            def _():
                give_z(k).start()

        repeat(4, lambda k: sum_y((z + 1 + k) % 4))
        q3[z] = t2[z]

    def give_x(k):
        return remote(s2, r3.at[x], p3_s.at[k], p3_r.at[x], (rep, (x + k) % 4 * 2 + c))

    def give_second(k):
        return remote(t3, ags.at[x], q4_s.at[k], q4_r.at[x], (rep, (tm + k) % 8))

    give_first = remote(ag, ag, p4_s, p4_r, sibling)
    @pl.when(owner)
    def _():
        repeat(3, lambda i: wait_for(r2a.at[peer_of(i, z)], p2a_r.at[peer_of(i, z)]))
        repeat(3, lambda i: wait_for(r2b.at[peer_of(i, y)], p2b_r.at[peer_of(i, y)]))
        s2[0] = four(r2a)
        s2[1] = four(r2b)
        repeat(3, lambda i: give_x(i + 1).start())
        r3[x] = s2[...]
        repeat(3, lambda i: wait_for(q3.at[peer_of(i, z)], q3_r.at[peer_of(i, z)]))
        t3[...] = four(q3)
        repeat(7, lambda i: give_second(i + 1).start())
        ags[x] = t3[...]
        repeat(3, lambda i: wait_for(r3.at[peer_of(i, x)], p3_r.at[peer_of(i, x)]))

        def sum_half(half):
            ag[half] = four(r3, half)

        repeat(2, sum_half)
        give_first.start()

    @pl.when(jnp.logical_not(owner))
    def _():
        give_first.wait_recv()

    write_first = pltpu.make_async_copy(ag, first_sums, out_sem.at[2])
    write_first.start()
    def from_rows(i):
        source = in_turn((tm + 1 + i) % 8)

        @pl.when(source != tm)
        def _():
            wait_for(pixel_rows(source), gi_r.at[source])

    repeat(8, from_rows)
    write_input = pltpu.make_async_copy(gout, input_out, out_sem.at[1])
    write_input.start()

    def take_sums(peer):
        @pl.when(jnp.logical_not(owner) | (peer != x))
        def _():
            wait_for(ags.at[peer], q4_r.at[peer])

    repeat(4, take_sums)

    write_second = pltpu.make_async_copy(ags, second_sums, out_sem.at[3])
    write_second.start()
    for copy in [give_ct, give_gp, give_sh, give_gph]:
        copy.wait_send()
    repeat(7, lambda i: spread(i).wait_send())
    repeat(7, lambda i: give_back(i).wait_send())
    repeat(9, lambda i: stop_x(i // 3, i % 3 + 1).wait_send())

    def drain_hand(source):
        hand_edge(source).wait_send()
        hand_rest(source).wait_send()

    repeat(8, drain_hand)

    def drain(shard, carry):
        delivered(source_f, shard)
        return carry

    lax.fori_loop(0, 8, drain, 0)

    def drain_y(i):
        @pl.when(2 * c + i != y)
        def _():
            give_y(i).wait_send()
            give_b(i).wait_send()

    repeat(2, drain_y)

    @pl.when(owner)
    def _():
        def drain_z(i):
            k = peer_of(i, z)
            give_a(k).wait_send()
            give_z(k).wait_send()
            give_x(i + 1).wait_send()

        repeat(3, drain_z)
        repeat(7, lambda i: give_second(i + 1).wait_send())
        give_first.wait_send()

    for write in (write_feat, write_input, write_first, write_second):
        write.wait()


def finish(features, grad_input, first, second, feat_out, input_out, first_out, second_out):
    feat_out[...] = features[...]
    input_out[...] = grad_input[...]
    scale_first = 1.0 / math.sqrt(131072)
    scale_second = 1.0 / math.sqrt(65536)
    for half in range(2):
        first_out[:, 128 * half : 128 * half + 128] = first[half].astype(f32) * scale_first
    for quarter in range(4):
        second_out[:, 128 * quarter : 128 * quarter + 128] = second[quarter].astype(f32) * scale_second


def body(video, frame_counts, first_weight, second_weight, cotangent):
    any_ = pl.BlockSpec(memory_space=pl.ANY)
    vmem = pltpu.VMEM
    dma = pltpu.SemaphoreType.DMA
    features, grad_input, first, second = pl.pallas_call(
        kernel,
        out_shape=(
            jax.ShapeDtypeStruct((8, 64, 512), bf16),
            jax.ShapeDtypeStruct((4, 512, 128), bf16),
            jax.ShapeDtypeStruct((2, ROWS_F, 128), bf16),
            jax.ShapeDtypeStruct((4, ROWS_S, 128), bf16),
        ),
        in_specs=[any_, pl.BlockSpec(memory_space=pltpu.SMEM), any_, any_, any_],
        out_specs=(any_,) * 4,
        scratch_shapes=[
            vmem((4, 512, 128), bf16),
            vmem((9, 768, 256), bf16),
            vmem((9, 768, 256), bf16),
            vmem((3, 512, 512), bf16),
            vmem((10, 64, 512), bf16),
            vmem((8, 64, 512), bf16),
            vmem((512, 1024), bf16),
            vmem((2, 576, 256), bf16),
            vmem((16, 192, 256), bf16),
            vmem((18, 6, 32, 768), bf16),
            vmem((1024, 256), f32),
            vmem((8, 2, 64, 256), bf16),
            vmem((2, 10, 64, 512), bf16),
            vmem((16, 4, 32, 256), bf16),
            vmem((16, 32, 256), bf16),
            vmem((256, 2048), bf16),
            vmem((18, 4, 32, 768), bf16),
            vmem((2, 3712, 128), bf16),
            vmem((4, 4, ROWS_F, 128), bf16),
            vmem((4, 2, ROWS_F, 128), bf16),
            vmem((4, ROWS_F, 128), bf16),
            vmem((2, ROWS_F, 128), bf16),
            vmem((4, ROWS_F, 128), bf16),
            vmem((4, ROWS_F, 128), bf16),
            vmem((2, ROWS_F, 128), bf16),
            vmem((4, 2, ROWS_F, 128), bf16),
            vmem((2, ROWS_F, 128), bf16),
            vmem((4, 768, 128), bf16),
            vmem((4, 768, 128), bf16),
            vmem((8, ROWS_S, 128), bf16),
            vmem((4, 4, ROWS_S, 128), bf16),
            vmem((4, ROWS_S, 128), bf16),
            vmem((4, ROWS_S, 128), bf16),
            vmem((ROWS_S, 128), bf16),
            vmem((4, ROWS_S, 128), bf16),
            vmem((8, 64, 512), bf16),
            vmem((8, 4, 64, 128), bf16),
            vmem((4, 512, 128), bf16),
            dma((4,)),
            dma((8,)), dma((8,)),
            dma((8,)), dma((8,)),
            dma((8,)), dma((8,)),
            dma, dma,
            dma, dma,
            dma, dma,
            dma, dma,
            dma((8,)), dma((8,)),
            dma((2, 8)), dma((4, 4)), dma((4, 2)),
            dma((4,)), dma((4,)), dma((2,)), dma((4,)),
            dma((4,)), dma((4,)),
            dma, dma,
            dma((3, 4)), dma((3, 4)),
            dma((2,)), dma((4,)),
            dma((4,)), dma((4,)),
            dma((8,)), dma((4,)),
            dma((4,)),
        ],
        compiler_params=pltpu.CompilerParams(
            collective_id=0, has_side_effects=True, vmem_limit_bytes=56 * 1024 * 1024
        ),
        cost_estimate=pl.CostEstimate(flops=14_000_000_000, bytes_accessed=9_000_000, transcendentals=500_000),
        name="window",
    )(
        video.reshape(4, 512, 128),
        frame_counts,
        first_weight.reshape(9, 768, 256),
        second_weight,
        cotangent.reshape(8, 64, 512),
    )
    features, grad_input, grad_first, grad_second = pl.pallas_call(
        finish,
        out_shape=(
            jax.ShapeDtypeStruct((8, 64, 512), bf16),
            jax.ShapeDtypeStruct((4, 512, 128), bf16),
            jax.ShapeDtypeStruct((432, 256), f32),
            jax.ShapeDtypeStruct((96, 512), f32),
        ),
        name="finish",
    )(features, grad_input, first, second)
    return (
        features.reshape(1, 8, 2, 32, 512),
        grad_input.reshape(1, 4, 16, 32, 128),
        grad_first,
        grad_second,
    )


def solution(mesh):
    placed = (
        P("rep", "tm", None, None, None),
        P("rep"),
        P(),
        P(),
        P("rep", None, "tm", None, None),
    )
    return jax.shard_map(
        body,
        mesh=mesh,
        in_specs=placed,
        out_specs=(
            P("rep", None, "tm", None, None),
            P("rep", "tm", None, None, None),
            P("rep", None),
            P("rep", None),
        ),
        check_vma=False,
    )
```

profile of v0, /device:TPU:1, one launch (start us, length us, event | category | flops | bytes accessed | tf_op | source)
XLA Modules:
  0.0 64.7 jit_solution(6849526037315610055)
XLA Ops:
  1.3 60.9 %window.1 = (bf16[8,64,512]{2,1,0:T(8,128)(2,1)}, bf16[4,512,128]{2,1,0:T(8,128)(2,1)}, bf16[2,432,128]{2,1,0:T(8,128)(2,1)}, bf16[4,96,128]{2,1,0:T(8,128)(2,1)}) custom-call(bf16[4,512,128]{2,1,0:T(8,128)(2,1)} %bitcast.6, s32[1]{0:T(128)S(6)} %copy.9.counts, bf16[9,768,256]{2,1,0:T(8,128)(2,1)} %bitcast.5, bf16[3,512,512]{2,1,0:T(8,128)(2,1)} %second_w.1, ...), custom_call_target="tpu_custom_call" | custom-call | flops 14000000000 | bytes 9000000 | tf_op jit(solution)/shard_map/window/pallas_call | solution.py:598
  62.2 2.5 %finish.1 = (bf16[8,64,512]{2,1,0:T(8,128)(2,1)}, bf16[4,512,128]{2,1,0:T(8,128)(2,1)}, f32[432,256]{1,0:T(8,128)}, f32[96,512]{1,0:T(8,128)}) custom-call(bf16[8,64,512]{2,1,0:T(8,128)(2,1)} %get-tuple-element.12.features, bf16[4,512,128]{2,1,0:T(8,128)(2,1)} %get-tuple-element.13.grad_input, bf16[2,432,128]{2,1,0:T(8,128)(2,1)} %get-tuple-element.14.first, ...), custom_call_target="tpu_custom_call" | custom-call | tf_op jit(solution)/shard_map/finish/pallas_call | solution.py:678
where the time goes:
time: 64.8 us; the launch traced here: 64.7 us
  Pallas kernels  63.4 us (98%)
  between operations  1.28 us (2%)
    pallas_call x1, Pallas kernels, body(): pl.pallas_call(kernel, out_shape=(jax.ShapeDtypeStruct((8, 64, 512), bf16...  60.9 us
    pallas_call x1, Pallas kernels, body(): pl.pallas_call(finish, out_shape=(jax.ShapeDtypeStruct((8, 64, 512), bf16...  2.48 us

commit v1 on v0

--- a/solution.py
+++ b/solution.py
@@ -75,9 +75,6 @@
         pltpu.make_async_copy(second_w, w2, load_sem.at[2]),
         pltpu.make_async_copy(first_w, w1, load_sem.at[3]),
     ]
-    for load in loads:
-        load.start()
-
     barrier = pltpu.get_barrier_semaphore()
 
     def greet(to):
@@ -86,6 +83,9 @@
     repeat(7, lambda i: greet((rep, (tm + 1 + i) % 8)))
     repeat(3, lambda i: greet(device(x, (y + 1 + i) % NY, z, c)))
     repeat(3, lambda i: greet(device(x, y, (z + 1 + i) % NZ, c)))
+
+    for load in loads:
+        load.start()
 
     live = counts[0]
     loads[0].wait()
@@ -284,15 +284,15 @@
     def source_f(half, shard):
         return pf.at[half, pl.ds(pl.multiple_of(128 + ROWS_F * shard, 16), ROWS_F)]
 
-    give_gp.wait_recv()
-    turn_rows(1 - c)
-
     def rest_from_sibling(source):
         block = win.at[frames_of(source), rest_rows(1 - c)]
         remote(block, block, fw_r.at[source], fw_r.at[source], sibling).wait_recv()
         take(source, 4 - 4 * c, 2)
 
     repeat(8, rest_from_sibling)
+
+    give_gp.wait_recv()
+    turn_rows(1 - c)
 
     def tap(j):
         k = 13 * c + j
@@ -307,15 +307,18 @@
 
     odd_row = y % 2
 
-    def send_shards(low):
-        repeat(4, lambda k: deliver(source_f, 4 * low + (z + 1 + k) % 4))
-
-    def first_taps(i, carry):
-        tap(6 * odd_row + i)
-        return carry
-
-    lax.fori_loop(0, 8, first_taps, 0, unroll=4)
-    send_shards(odd_row)
+    def in_order(index, last):
+        return last * odd_row + (1 - 2 * odd_row) * index
+
+    def send_pair(pair):
+        repeat(2, lambda k: deliver(source_f, in_order(2 * pair + (z + k) % 2, 7)))
+
+    def first_taps(n):
+        for i in range(4):
+            tap(in_order(4 * n + i, 13))
+        send_pair(n)
+
+    repeat(2, first_taps)
 
     give_ct.wait_recv()
     ct_t[:, 512:1024] = cts[...].reshape(512, 512).T
@@ -341,12 +344,12 @@
     repeat(3, second_rows)
     q1[x] = px[x]
 
-    def last_taps(i, carry):
-        tap(8 - 8 * odd_row + i)
-        return carry
-
-    lax.fori_loop(0, 6, last_taps, 0, unroll=3)
-    send_shards(1 - odd_row)
+    def last_taps(n):
+        for i in range(3):
+            tap(in_order(8 + 3 * n + i, 13))
+        send_pair(2 + n)
+
+    repeat(2, last_taps)
 
     give_gph.wait_recv()
     inner = jnp.where((c == 0) & (x == 0) | (c == 1) & (x == 3), 0.0, 1.0).astype(bf16)
@@ -485,39 +488,28 @@
         repeat(4, lambda k: sum_y((z + 1 + k) % 4))
         q3[z] = t2[z]
 
-    def give_x(k):
-        return remote(s2, r3.at[x], p3_s.at[k], p3_r.at[x], (rep, (x + k) % 4 * 2 + c))
+    def give_x(half, k):
+        slot = r3.at[x, half]
+        return remote(s2.at[half], slot, p3_s.at[half, k], p3_r.at[half, x], (rep, (x + k) % 4 * 2 + c))
 
     def give_second(k):
         return remote(t3, ags.at[x], q4_s.at[k], q4_r.at[x], (rep, (tm + k) % 8))
 
-    give_first = remote(ag, ag, p4_s, p4_r, sibling)
+    def give_first(half):
+        return remote(ag.at[half], ag.at[half], p4_s.at[half], p4_r.at[half], sibling)
+
     @pl.when(owner)
     def _():
-        repeat(3, lambda i: wait_for(r2a.at[peer_of(i, z)], p2a_r.at[peer_of(i, z)]))
-        repeat(3, lambda i: wait_for(r2b.at[peer_of(i, y)], p2b_r.at[peer_of(i, y)]))
-        s2[0] = four(r2a)
-        s2[1] = four(r2b)
-        repeat(3, lambda i: give_x(i + 1).start())
+        for half, slots, sems, home in ((0, r2a, p2a_r, z), (1, r2b, p2b_r, y)):
+            repeat(3, lambda i: wait_for(slots.at[peer_of(i, home)], sems.at[peer_of(i, home)]))
+            s2[half] = four(slots)
+            repeat(3, lambda i: give_x(half, i + 1).start())
         r3[x] = s2[...]
         repeat(3, lambda i: wait_for(q3.at[peer_of(i, z)], q3_r.at[peer_of(i, z)]))
         t3[...] = four(q3)
         repeat(7, lambda i: give_second(i + 1).start())
         ags[x] = t3[...]
-        repeat(3, lambda i: wait_for(r3.at[peer_of(i, x)], p3_r.at[peer_of(i, x)]))
-
-        def sum_half(half):
-            ag[half] = four(r3, half)
-
-        repeat(2, sum_half)
-        give_first.start()
-
-    @pl.when(jnp.logical_not(owner))
-    def _():
-        give_first.wait_recv()
-
-    write_first = pltpu.make_async_copy(ag, first_sums, out_sem.at[2])
-    write_first.start()
+
     def from_rows(i):
         source = in_turn((tm + 1 + i) % 8)
 
@@ -529,15 +521,6 @@
     write_input = pltpu.make_async_copy(gout, input_out, out_sem.at[1])
     write_input.start()
 
-    def take_sums(peer):
-        @pl.when(jnp.logical_not(owner) | (peer != x))
-        def _():
-            wait_for(ags.at[peer], q4_r.at[peer])
-
-    repeat(4, take_sums)
-
-    write_second = pltpu.make_async_copy(ags, second_sums, out_sem.at[3])
-    write_second.start()
     for copy in [give_ct, give_gp, give_sh, give_gph]:
         copy.wait_send()
     repeat(7, lambda i: spread(i).wait_send())
@@ -549,12 +532,7 @@
         hand_rest(source).wait_send()
 
     repeat(8, drain_hand)
-
-    def drain(shard, carry):
-        delivered(source_f, shard)
-        return carry
-
-    lax.fori_loop(0, 8, drain, 0)
+    repeat(8, lambda shard: delivered(source_f, shard))
 
     def drain_y(i):
         @pl.when(2 * c + i != y)
@@ -570,11 +548,36 @@
             k = peer_of(i, z)
             give_a(k).wait_send()
             give_z(k).wait_send()
-            give_x(i + 1).wait_send()
 
         repeat(3, drain_z)
+        def sum_half(half):
+            repeat(3, lambda i: wait_for(r3.at[peer_of(i, x), half], p3_r.at[half, peer_of(i, x)]))
+            ag[half] = four(r3, half)
+            give_first(half).start()
+
+        repeat(2, sum_half)
+
+    @pl.when(jnp.logical_not(owner))
+    def _():
+        repeat(2, lambda half: give_first(half).wait_recv())
+
+    write_first = pltpu.make_async_copy(ag, first_sums, out_sem.at[2])
+    write_first.start()
+
+    def take_sums(peer):
+        @pl.when(jnp.logical_not(owner) | (peer != x))
+        def _():
+            wait_for(ags.at[peer], q4_r.at[peer])
+
+    repeat(4, take_sums)
+    write_second = pltpu.make_async_copy(ags, second_sums, out_sem.at[3])
+    write_second.start()
+
+    @pl.when(owner)
+    def _():
+        repeat(6, lambda i: give_x(i // 3, i % 3 + 1).wait_send())
         repeat(7, lambda i: give_second(i + 1).wait_send())
-        give_first.wait_send()
+        repeat(2, lambda half: give_first(half).wait_send())
 
     for write in (write_feat, write_input, write_first, write_second):
         write.wait()
@@ -655,8 +658,8 @@
             dma((8,)), dma((8,)),
             dma((2, 8)), dma((4, 4)), dma((4, 2)),
             dma((4,)), dma((4,)), dma((2,)), dma((4,)),
-            dma((4,)), dma((4,)),
-            dma, dma,
+            dma((2, 4)), dma((2, 4)),
+            dma((2,)), dma((2,)),
             dma((3, 4)), dma((3, 4)),
             dma((2,)), dma((4,)),
             dma((4,)), dma((4,)),

time: 64.8 us -> 62.6 us (0.966)
  Pallas kernels: 63.4 us -> 61.2 us
    pallas_call x1, Pallas kernels: 60.9 us -> 58.7 us  [body(): pl.pallas_call(kernel, out_shape=(jax.ShapeDtypeStruct((8, 64, 512), bf16...]
where the time goes in v1:
time: 62.6 us; the launch traced here: 62.5 us
  Pallas kernels  61.2 us (98%)
  between operations  1.28 us (2%)
    pallas_call x1, Pallas kernels, body(): pl.pallas_call(kernel, out_shape=(jax.ShapeDtypeStruct((8, 64, 512), bf16...  58.7 us
    pallas_call x1, Pallas kernels, body(): pl.pallas_call(finish, out_shape=(jax.ShapeDtypeStruct((8, 64, 512), bf16...  2.48 us

profile of v1, /device:TPU:1, one launch (start us, length us, event | category | flops | bytes accessed | tf_op | source)
XLA Modules:
  0.0 62.5 jit_solution(6477256954250067980)
XLA Ops:
  1.3 58.7 %window.1 = (bf16[8,64,512]{2,1,0:T(8,128)(2,1)}, bf16[4,512,128]{2,1,0:T(8,128)(2,1)}, bf16[2,432,128]{2,1,0:T(8,128)(2,1)}, bf16[4,96,128]{2,1,0:T(8,128)(2,1)}) custom-call(bf16[4,512,128]{2,1,0:T(8,128)(2,1)} %bitcast.6, s32[1]{0:T(128)S(6)} %copy.9.counts, bf16[9,768,256]{2,1,0:T(8,128)(2,1)} %bitcast.5, bf16[3,512,512]{2,1,0:T(8,128)(2,1)} %second_w.1, ...), custom_call_target="tpu_custom_call" | custom-call | flops 14000000000 | bytes 9000000 | tf_op jit(solution)/shard_map/window/pallas_call | solution.py:601
  60.0 2.5 %finish.1 = (bf16[8,64,512]{2,1,0:T(8,128)(2,1)}, bf16[4,512,128]{2,1,0:T(8,128)(2,1)}, f32[432,256]{1,0:T(8,128)}, f32[96,512]{1,0:T(8,128)}) custom-call(bf16[8,64,512]{2,1,0:T(8,128)(2,1)} %get-tuple-element.12.features, bf16[4,512,128]{2,1,0:T(8,128)(2,1)} %get-tuple-element.13.grad_input, bf16[2,432,128]{2,1,0:T(8,128)(2,1)} %get-tuple-element.14.first, ...), custom_call_target="tpu_custom_call" | custom-call | tf_op jit(solution)/shard_map/finish/pallas_call | solution.py:681

commit v2 on v1

--- a/solution.py
+++ b/solution.py
@@ -313,16 +313,6 @@
     def send_pair(pair):
         repeat(2, lambda k: deliver(source_f, in_order(2 * pair + (z + k) % 2, 7)))
 
-    def first_taps(n):
-        for i in range(4):
-            tap(in_order(4 * n + i, 13))
-        send_pair(n)
-
-    repeat(2, first_taps)
-
-    give_ct.wait_recv()
-    ct_t[:, 512:1024] = cts[...].reshape(512, 512).T
-    give_sh.wait_recv()
 
     def stop_x(n, k):
         to = (x + k) % 4
@@ -341,7 +331,22 @@
             px[to_x, at] = turned[:, 128 * to_x : 128 * to_x + 128]
         repeat(3, lambda k: stop_x(n, k + 1).start())
 
-    repeat(3, second_rows)
+    def second_taps():
+        give_ct.wait_recv()
+        ct_t[:, 512:1024] = cts[...].reshape(512, 512).T
+        give_sh.wait_recv()
+        repeat(3, second_rows)
+
+    def first_taps(n):
+        for i in range(4):
+            tap(in_order(4 * n + i, 13))
+        send_pair(n)
+
+        @pl.when(n == 0)
+        def _():
+            second_taps()
+
+    repeat(2, first_taps)
     q1[x] = px[x]
 
     def last_taps(n):
@@ -503,7 +508,7 @@
         for half, slots, sems, home in ((0, r2a, p2a_r, z), (1, r2b, p2b_r, y)):
             repeat(3, lambda i: wait_for(slots.at[peer_of(i, home)], sems.at[peer_of(i, home)]))
             s2[half] = four(slots)
-            repeat(3, lambda i: give_x(half, i + 1).start())
+            repeat(3, lambda i: give_x(half, (i + 1) % 3 + 1).start())
         r3[x] = s2[...]
         repeat(3, lambda i: wait_for(q3.at[peer_of(i, z)], q3_r.at[peer_of(i, z)]))
         t3[...] = four(q3)

time: 62.6 us -> 61.3 us (0.979)
  Pallas kernels: 61.2 us -> 59.9 us
    pallas_call x1, Pallas kernels: 58.7 us -> 57.4 us  [body(): pl.pallas_call(kernel, out_shape=(jax.ShapeDtypeStruct((8, 64, 512), bf16...]
where the time goes in v2:
time: 61.3 us; the launch traced here: 61.2 us
  Pallas kernels  59.9 us (98%)
  between operations  1.28 us (2%)
    pallas_call x1, Pallas kernels, body(): pl.pallas_call(kernel, out_shape=(jax.ShapeDtypeStruct((8, 64, 512), bf16...  57.4 us
    pallas_call x1, Pallas kernels, body(): pl.pallas_call(finish, out_shape=(jax.ShapeDtypeStruct((8, 64, 512), bf16...  2.48 us

profile of v2, /device:TPU:1, one launch (start us, length us, event | category | flops | bytes accessed | tf_op | source)
XLA Modules:
  0.0 61.2 jit_solution(12173007756060713523)
XLA Ops:
  1.3 57.4 %window.1 = (bf16[8,64,512]{2,1,0:T(8,128)(2,1)}, bf16[4,512,128]{2,1,0:T(8,128)(2,1)}, bf16[2,432,128]{2,1,0:T(8,128)(2,1)}, bf16[4,96,128]{2,1,0:T(8,128)(2,1)}) custom-call(bf16[4,512,128]{2,1,0:T(8,128)(2,1)} %bitcast.6, s32[1]{0:T(128)S(6)} %copy.9.counts, bf16[9,768,256]{2,1,0:T(8,128)(2,1)} %bitcast.5, bf16[3,512,512]{2,1,0:T(8,128)(2,1)} %second_w.1, ...), custom_call_target="tpu_custom_call" | custom-call | flops 14000000000 | bytes 9000000 | tf_op jit(solution)/shard_map/window/pallas_call | solution.py:606
  58.7 2.5 %finish.1 = (bf16[8,64,512]{2,1,0:T(8,128)(2,1)}, bf16[4,512,128]{2,1,0:T(8,128)(2,1)}, f32[432,256]{1,0:T(8,128)}, f32[96,512]{1,0:T(8,128)}) custom-call(bf16[8,64,512]{2,1,0:T(8,128)(2,1)} %get-tuple-element.12.features, bf16[4,512,128]{2,1,0:T(8,128)(2,1)} %get-tuple-element.13.grad_input, bf16[2,432,128]{2,1,0:T(8,128)(2,1)} %get-tuple-element.14.first, ...), custom_call_target="tpu_custom_call" | custom-call | tf_op jit(solution)/shard_map/finish/pallas_call | solution.py:686

commit v3 on v2

--- a/solution.py
+++ b/solution.py
@@ -329,7 +329,7 @@
         at = pl.ds(pl.multiple_of(256 * n, 256), 256)
         for to_x in range(4):
             px[to_x, at] = turned[:, 128 * to_x : 128 * to_x + 128]
-        repeat(3, lambda k: stop_x(n, k + 1).start())
+        repeat(3, lambda k: stop_x(n, (k + 1) % 3 + 1).start())
 
     def second_taps():
         give_ct.wait_recv()
@@ -408,7 +408,6 @@
         n, peer = i // 3, peer_of(i % 3, x)
         wait_for(q1.at[peer, pl.ds(pl.multiple_of(256 * n, 256), 256)], q1_r.at[n, peer])
 
-    repeat(9, from_x)
 
     def four(ref, *index):
         total = ref[(0,) + index].astype(f32)
@@ -420,7 +419,6 @@
         t1[i] = four(q1, pl.ds(pl.multiple_of(96 * i, 16), 96))
         return carry
 
-    lax.fori_loop(0, 8, sum_x, 0)
 
     def give_y(i):
         return remote(
@@ -436,7 +434,6 @@
         def _():
             q2[y] = t1[pl.ds(4 * i, 4)]
 
-    repeat(2, start_y)
 
     def landed(slot, sem):
         pltpu.make_async_copy(slot, slot, sem).wait()
@@ -463,6 +460,9 @@
             r2b[y] = s1b[i]
 
     sum_b(odd_row)
+    repeat(9, from_x)
+    lax.fori_loop(0, 8, sum_x, 0)
+    repeat(2, start_y)
 
     @pl.when(owner)
     def _():

time: 61.3 us -> 61.4 us (level)
  no operation moved by 1% of the time
where the time goes in v3:
time: 61.4 us; the launch traced here: 61.3 us
  Pallas kernels  60 us (98%)
  between operations  1.28 us (2%)
    pallas_call x1, Pallas kernels, body(): pl.pallas_call(kernel, out_shape=(jax.ShapeDtypeStruct((8, 64, 512), bf16...  57.5 us
    pallas_call x1, Pallas kernels, body(): pl.pallas_call(finish, out_shape=(jax.ShapeDtypeStruct((8, 64, 512), bf16...  2.48 us

profile of v3, /device:TPU:1, one launch (start us, length us, event | category | flops | bytes accessed | tf_op | source)
XLA Modules:
  0.0 61.3 jit_solution(9936572881546819843)
XLA Ops:
  1.3 57.5 %window.1 = (bf16[8,64,512]{2,1,0:T(8,128)(2,1)}, bf16[4,512,128]{2,1,0:T(8,128)(2,1)}, bf16[2,432,128]{2,1,0:T(8,128)(2,1)}, bf16[4,96,128]{2,1,0:T(8,128)(2,1)}) custom-call(bf16[4,512,128]{2,1,0:T(8,128)(2,1)} %bitcast.6, s32[1]{0:T(128)S(6)} %copy.9.counts, bf16[9,768,256]{2,1,0:T(8,128)(2,1)} %bitcast.5, bf16[3,512,512]{2,1,0:T(8,128)(2,1)} %second_w.1, ...), custom_call_target="tpu_custom_call" | custom-call | flops 14000000000 | bytes 9000000 | tf_op jit(solution)/shard_map/window/pallas_call | solution.py:606
  58.8 2.5 %finish.1 = (bf16[8,64,512]{2,1,0:T(8,128)(2,1)}, bf16[4,512,128]{2,1,0:T(8,128)(2,1)}, f32[432,256]{1,0:T(8,128)}, f32[96,512]{1,0:T(8,128)}) custom-call(bf16[8,64,512]{2,1,0:T(8,128)(2,1)} %get-tuple-element.12.features, bf16[4,512,128]{2,1,0:T(8,128)(2,1)} %get-tuple-element.13.grad_input, bf16[2,432,128]{2,1,0:T(8,128)(2,1)} %get-tuple-element.14.first, ...), custom_call_target="tpu_custom_call" | custom-call | tf_op jit(solution)/shard_map/finish/pallas_call | solution.py:686
